TPU v7x, 512 devices: a whole 4x8x8 slice. The times are simulated.
512 devices in a mesh: band: 16 (over z, core), tile: 32 (over y, x).
Axes of the slice: x: 4, y: 8, z: 8, core: 2. Of those that a mesh axis runs over, the one named last changes fastest.
Arguments:
- sources: bfloat16 [524288, 256], P(('band', 'tile')), may hold values from -6 to 6
- observed: bfloat16 [8192, 256], P('tile'), may hold values from -6 to 6
- v_factors: bfloat16 [8, 96, 524288], P(None, None, ('band', 'tile')), may hold values from -0.1875 to 0.1875
- u_factors: bfloat16 [512, 96, 8192], P('band', None, 'tile'), may hold values from -0.03125 to 0.03125
- tile_ranks: int32 [8, 512], P(None, ('band', 'tile')), may hold values from 32 to 96
- v_exponents: int32 [8, 512], P(None, ('band', 'tile')), may hold values from -1 to 1
- u_exponents: int32 [8, 512], P(None, ('band', 'tile')), may hold values from -1 to 1
Outputs:
- residual: float32 [8192, 256], P('tile', 'band')
- gradient: bfloat16 [524288, 256], P(('band', 'tile'))
All inputs are finite; a program needn't handle non-finite values.
Results may differ from a plain program's by a relative error of at most 0.012.
Values may be sent and summed in bfloat16 or wider, within the bound.
A program may use at most 64 MiB of HBM per device.

v0:
```python
import jax
import jax.numpy as jnp
from jax import lax
from jax.sharding import PartitionSpec as P


def local(sources, observed, v_factors, u_factors, tile_ranks, v_exponents, u_exponents):
    tile_count = lax.axis_size("tile")
    band_count = lax.axis_size("band")
    row_tiles = v_factors.shape[0]
    rank_max = v_factors.shape[1]
    slices_per = tile_count // row_tiles
    rank_index = jnp.arange(rank_max, dtype=jnp.int32)
    weight = (rank_index[None, :] < tile_ranks).astype(jnp.float32)
    weight = weight * jnp.exp2((v_exponents + u_exponents).astype(jnp.float32))
    products = jnp.einsum("ikb,bs->iks", v_factors, sources, preferred_element_type=jnp.float32)
    pieces = (products * weight[:, :, None]).astype(jnp.bfloat16)
    outgoing = jnp.repeat(pieces, slices_per, axis=0)
    incoming = lax.all_to_all(outgoing, "tile", split_axis=0, concat_axis=0, tiled=True)
    partial_value = jnp.einsum(
        "ukh,uks->hs", u_factors, incoming, preferred_element_type=jnp.float32
    )
    col_width = observed.shape[1] // band_count
    offset = lax.axis_index("band") * col_width
    totals = lax.psum(partial_value, "band")
    full_rows = totals - observed.astype(jnp.float32)
    residual = lax.dynamic_slice_in_dim(full_rows, offset, col_width, 1)
    residual_rows = full_rows.astype(jnp.bfloat16)
    adjoint_part = jnp.einsum(
        "ukh,hs->uks", u_factors, residual_rows, preferred_element_type=jnp.float32
    )
    returned = lax.all_to_all(
        adjoint_part.astype(jnp.bfloat16), "tile", split_axis=0, concat_axis=0, tiled=True
    )
    summed = (
        returned.astype(jnp.float32)
        .reshape(row_tiles, slices_per, rank_max, returned.shape[2])
        .sum(axis=1)
    )
    adjoint = (summed * weight[:, :, None]).astype(jnp.bfloat16)
    gradient = jnp.einsum("ikb,iks->bs", v_factors, adjoint, preferred_element_type=jnp.float32)
    return (residual, gradient.astype(jnp.bfloat16))


def solution(mesh):
    in_specs = (
        P(("band", "tile"), None),
        P("tile", None),
        P(None, None, ("band", "tile")),
        P("band", None, "tile"),
        P(None, ("band", "tile")),
        P(None, ("band", "tile")),
        P(None, ("band", "tile")),
    )
    out_specs = (P("tile", "band"), P(("band", "tile"), None))
    return jax.shard_map(local, mesh=mesh, in_specs=in_specs, out_specs=out_specs, check_vma=False)
```

profile of v0, /device:TPU:4, one launch (start us, length us, event | category | flops | bytes accessed | tf_op | source)
XLA Modules:
  0.0 238.3 jit_solution(13547615035790127038)
XLA Ops:
  7.2 0.0 copy-start
  7.2 0.0 all-reduce.2.cloned.1.call-start
  7.2 0.8 exponential_bitcast_fusion
  8.0 0.7 fusion.8
  8.7 2.1 fusion.2
  10.8 0.2 broadcast_in_dim.2
  11.0 49.3 %all_to_all.10 = bf16[32,96,256]{2,1,0:T(8,128)(2,1)S(1)} all-to-all(bf16[32,96,256]{2,1,0:T(8,128)(2,1)S(1)} %bitcast.32), channel_id=1, replica_groups=mesh['band'=16,'tile'=32] {'tile'}, dimensions={0} | all-to-all | bytes 3145728 | tf_op jit(solution)/shard_map/all_to_all | solution.py:19
  60.3 0.0 copy-done
  60.3 0.0 copy-start.1
  60.3 1.3 convolution_bitcast_fusion.1
  61.7 0.0 all-reduce.2.cloned.1.call-update
  61.7 0.0 copy-done.1
  61.7 0.1 copy.9
  61.8 114.5 %all-reduce.2.cloned.1.call-done = f32[256,256]{0,1:T(8,128)} async-done(((f32[256,256]{0,1:T(8,128)}), f32[256,256]{0,1:T(8,128)}) %all-reduce.2.cloned.1.call-update) | async-done | bytes 262160 | tf_op jit(solution)/shard_map/psum | solution.py:25
  176.3 1.0 convert_subtract_fusion
  177.3 1.8 fusion
  179.1 9.9 %all-to-all-start.1 = ((bf16[32,96,256]{2,1,0:T(8,128)(2,1)}), bf16[32,96,256]{2,1,0:T(8,128)(2,1)S(1)}, u32[]{:S(2)}, u32[]{:S(2)}) async-start(bf16[32,96,256]{2,1,0:T(8,128)(2,1)} %fusion), calls=%async_computation.1 | async-start | bytes 3145728 | tf_op jit(solution)/shard_map/all_to_all | solution.py:32
  189.0 0.6 constant_dynamic-slice_fusion
  189.6 38.7 %all-to-all-done.1 = bf16[32,96,256]{2,1,0:T(8,128)(2,1)S(1)} async-done(((bf16[32,96,256]{2,1,0:T(8,128)(2,1)}), bf16[32,96,256]{2,1,0:T(8,128)(2,1)S(1)}, u32[]{:S(2)}, u32[]{:S(2)}) %all-to-all-start.1) | async-done | bytes 1572896 | tf_op jit(solution)/shard_map/all_to_all | solution.py:32
  228.3 0.0 copy-start.2
  228.3 0.2 convert_reduce_fusion
  228.5 1.2 copy-done.2
  229.7 0.7 fusion.3
  230.4 1.0 copy.11
Async XLA Ops:
  7.2 53.2 %copy-start = (bf16[32,96,256]{2,1,0:T(8,128)(2,1)S(1)}, bf16[32,96,256]{2,1,0:T(8,128)(2,1)}, u32[]{:S(2)}) copy-start(bf16[32,96,256]{2,1,0:T(8,128)(2,1)} %param.10) | copy-start | bytes 4718596
  7.2 169.2 %all-reduce.2.cloned.1.call-start = ((), (), s32[]{:S(2)}) async-start(), calls=%async_computation.2 | async-start | bytes 524288 | tf_op jit(solution)/shard_map/psum | solution.py:25
  60.3 1.3 copy-start.1
  179.1 49.2 %all-to-all-start.1 = ((bf16[32,96,256]{2,1,0:T(8,128)(2,1)}), bf16[32,96,256]{2,1,0:T(8,128)(2,1)S(1)}, u32[]{:S(2)}, u32[]{:S(2)}) async-start(bf16[32,96,256]{2,1,0:T(8,128)(2,1)} %fusion), calls=%async_computation.1 | async-start | bytes 3145728 | tf_op jit(solution)/shard_map/all_to_all | solution.py:32
  228.3 1.4 copy-start.2
Sparse Core Ops, SparseCore 0:
  61.8 114.4 all-reduce.1
where the time goes:
time: 239 us; the launch traced here: 238 us
  waiting for transfers between devices  153 us (64%)
  blocking collectives  49.3 us (21%)
  between operations  14.1 us (6%)
  starting transfers between devices  9.9 us (4%)
  matrix products  5.87 us (2%)
  local copies, waits for them, and re-layouts  3.08 us (1%)
  other arithmetic  2.71 us (1%)
    psum x1, waiting for transfers between devices, local(): totals = lax.psum(partial_value, 'band')  115 us
    all_to_all x1, blocking collectives, local(): lax.all_to_all(outgoing, 'tile', split_axis=0, concat_axis=0, tiled=True)  49.3 us
    all_to_all x1, waiting for transfers between devices, local(): lax.all_to_all(adjoint_part.astype(jnp.bfloat16), 'tile', split_axis=0, c...  38.7 us
    all_to_all x1, starting transfers between devices, local(): lax.all_to_all(adjoint_part.astype(jnp.bfloat16), 'tile', split_axis=0, c...  9.86 us
  transfers between devices with their start and end apart: 2, of which 2 were waited for; matrix products, arithmetic and copies ran while one was open for 0% of the time, Pallas kernels for 0%

commit v1 on v0

--- a/solution.py
+++ b/solution.py
@@ -22,7 +22,11 @@
     )
     col_width = observed.shape[1] // band_count
     offset = lax.axis_index("band") * col_width
-    totals = lax.psum(partial_value, "band")
+    devices = lax.axis_size("band")
+    totals, far = (partial_value, 1)
+    while far < devices:
+        totals = totals + lax.ppermute(totals, "band", [(i, i ^ far) for i in range(devices)])
+        far = 2 * far
     full_rows = totals - observed.astype(jnp.float32)
     residual = lax.dynamic_slice_in_dim(full_rows, offset, col_width, 1)
     residual_rows = full_rows.astype(jnp.bfloat16)

time: 239 us -> 154 us (0.64)
  the two profiles are of different devices: /device:TPU:4 before, /device:TPU:194 now
where the time goes in v1:
time: 154 us
  waiting for transfers between devices  74 us (48%)
  blocking collectives  49.4 us (32%)
  starting transfers between devices  19.7 us (13%)
  matrix products  5.15 us (3%)
  local copies, waits for them, and re-layouts  3.08 us (2%)
  other arithmetic  1.89 us (1%)
    all_to_all x1, blocking collectives, local(): lax.all_to_all(outgoing, 'tile', split_axis=0, concat_axis=0, tiled=True)  49.4 us
    all_to_all x1, waiting for transfers between devices, local(): lax.all_to_all(adjoint_part.astype(jnp.bfloat16), 'tile', split_axis=0, c...  38.2 us
    ppermute x4, waiting for transfers between devices, local(): lax.ppermute(totals, 'band', [(i, i ^ far) for i in range(devices)])  35.8 us
    ppermute x4, starting transfers between devices, local(): lax.ppermute(totals, 'band', [(i, i ^ far) for i in range(devices)])  14.1 us
    all_to_all x1, starting transfers between devices, local(): lax.all_to_all(adjoint_part.astype(jnp.bfloat16), 'tile', split_axis=0, c...  5.57 us
  transfers between devices with their start and end apart: 5, of which 5 were waited for; matrix products, arithmetic and copies ran while one was open for 0% of the time, Pallas kernels for 0%

profile of v1, /device:TPU:194, one launch (start us, length us, event | category | flops | bytes accessed | tf_op | source)
XLA Modules:
  0.0 154.0 jit_solution(17842790024862163306)
XLA Ops:
  0.6 0.0 copy-start
  0.6 0.8 exponential_bitcast_fusion
  1.4 0.7 fusion.8
  2.2 2.1 %fusion.2 = bf16[8,96,256]{2,1,0:T(8,128)(2,1)S(1)} fusion(bf16[8,96,1024]{2,1,0:T(8,128)(2,1)} %param.9, bf16[1024,256]{1,0:T(8,128)(2,1)} %param.7, f32[8,96]{1,0:T(8,128)S(1)} %fusion.8), kind=kOutput, calls=%fused_computation.6 | convolution fusion | flops 403046400 | bytes 2493440 | tf_op jit(solution)/shard_map/ikb,bs->iks/dot_general | solution.py:16
  4.3 0.2 broadcast_in_dim.2
  4.4 49.4 %all_to_all.10 = bf16[32,96,256]{2,1,0:T(8,128)(2,1)S(1)} all-to-all(bf16[32,96,256]{2,1,0:T(8,128)(2,1)S(1)} %bitcast.32), channel_id=1, replica_groups=mesh['band'=16,'tile'=32] {'tile'}, dimensions={0} | all-to-all | bytes 3145728 | tf_op jit(solution)/shard_map/all_to_all | solution.py:19
  53.8 0.6 convolution_bitcast_fusion.1
  54.4 2.1 %collective-permute-start = (f32[256,256]{0,1:T(8,128)S(1)}, f32[256,256]{0,1:T(8,128)S(1)}, u32[]{:S(2)}, u32[]{:S(2)}) collective-permute-start(f32[256,256]{0,1:T(8,128)S(1)} %convolution_bitcast_fusion.1), channel_id=1, source_target_pairs={{0,32},{32,0},{64,96},{96,64},{128,160},{160,128},{192,224},{224,1... | collective-permute-start | bytes 786440 | tf_op jit(solution)/shard_map/ppermute | solution.py:28
  56.5 1.5 collective-permute-done
  58.0 1.9 %collective-permute-start.1 = (f32[256,256]{0,1:T(8,128)S(1)}, f32[256,256]{0,1:T(8,128)S(1)}, u32[]{:S(2)}, u32[]{:S(2)}) collective-permute-start(f32[256,256]{0,1:T(8,128)S(1)} %add.19), channel_id=1, source_target_pairs={{0,64},{32,96},{64,0},{96,32},{128,192},{160,224},{192,128},{224,1... | collective-permute-start | bytes 786440 | tf_op jit(solution)/shard_map/ppermute | solution.py:28
  60.0 8.3 %collective-permute-done.1 = f32[256,256]{0,1:T(8,128)S(1)} collective-permute-done((f32[256,256]{0,1:T(8,128)S(1)}, f32[256,256]{0,1:T(8,128)S(1)}, u32[]{:S(2)}, u32[]{:S(2)}) %collective-permute-start.1) | collective-permute-done | bytes 262176 | tf_op jit(solution)/shard_map/ppermute | solution.py:28
  68.3 1.9 %collective-permute-start.2 = (f32[256,256]{0,1:T(8,128)S(1)}, f32[256,256]{0,1:T(8,128)S(1)}, u32[]{:S(2)}, u32[]{:S(2)}) collective-permute-start(f32[256,256]{0,1:T(8,128)S(1)} %add.20), channel_id=1, source_target_pairs={{0,128},{32,160},{64,192},{96,224},{128,0},{160,32},{192,64},{224,... | collective-permute-start | bytes 786440 | tf_op jit(solution)/shard_map/ppermute | solution.py:28
  70.2 14.0 %collective-permute-done.2 = f32[256,256]{0,1:T(8,128)S(1)} collective-permute-done((f32[256,256]{0,1:T(8,128)S(1)}, f32[256,256]{0,1:T(8,128)S(1)}, u32[]{:S(2)}, u32[]{:S(2)}) %collective-permute-start.2) | collective-permute-done | bytes 262176 | tf_op jit(solution)/shard_map/ppermute | solution.py:28
  84.3 8.3 %collective-permute-start.3 = (f32[256,256]{0,1:T(8,128)S(1)}, f32[256,256]{0,1:T(8,128)S(1)}, u32[]{:S(2)}, u32[]{:S(2)}) collective-permute-start(f32[256,256]{0,1:T(8,128)S(1)} %add.21), channel_id=1, source_target_pairs={{0,256},{32,288},{64,320},{96,352},{128,384},{160,416},{192,448},{... | collective-permute-start | bytes 786440 | tf_op jit(solution)/shard_map/ppermute | solution.py:28
  92.5 0.1 copy.9
  92.7 12.0 %collective-permute-done.3 = f32[256,256]{0,1:T(8,128)S(1)} collective-permute-done((f32[256,256]{0,1:T(8,128)S(1)}, f32[256,256]{0,1:T(8,128)S(1)}, u32[]{:S(2)}, u32[]{:S(2)}) %collective-permute-start.3) | collective-permute-done | bytes 262176 | tf_op jit(solution)/shard_map/ppermute | solution.py:28
  104.7 1.8 %fusion = bf16[32,96,256]{2,1,0:T(8,128)(2,1)} fusion(bf16[32,96,256]{2,1,0:T(8,128)(2,1)S(1)} %copy-done, f32[256,256]{0,1:T(8,128)S(1)} %convert_subtract_fusion), kind=kOutput, calls=%fused_computation.2 | convolution fusion | flops 403505152 | bytes 3407872 | tf_op jit(solution)/shard_map/ukh,hs->uks/dot_general | solution.py:33
  106.4 5.6 %all-to-all-start.1 = ((bf16[32,96,256]{2,1,0:T(8,128)(2,1)}), bf16[32,96,256]{2,1,0:T(8,128)(2,1)S(1)}, u32[]{:S(2)}, u32[]{:S(2)}) async-start(bf16[32,96,256]{2,1,0:T(8,128)(2,1)} %fusion), calls=%async_computation.1 | async-start | bytes 3145728 | tf_op jit(solution)/shard_map/all_to_all | solution.py:36
  112.0 0.6 constant_dynamic-slice_fusion
  112.6 38.2 %all-to-all-done.1 = bf16[32,96,256]{2,1,0:T(8,128)(2,1)S(1)} async-done(((bf16[32,96,256]{2,1,0:T(8,128)(2,1)}), bf16[32,96,256]{2,1,0:T(8,128)(2,1)S(1)}, u32[]{:S(2)}, u32[]{:S(2)}) %all-to-all-start.1) | async-done | bytes 1572896 | tf_op jit(solution)/shard_map/all_to_all | solution.py:36
  150.9 0.2 convert_reduce_fusion
  151.1 1.2 copy-done.2
  152.3 0.7 fusion.3
  153.0 1.0 copy.11
  (8 shorter events, 0.2 us)
Async XLA Ops:
  0.6 53.2 %copy-start = (bf16[32,96,256]{2,1,0:T(8,128)(2,1)S(1)}, bf16[32,96,256]{2,1,0:T(8,128)(2,1)}, u32[]{:S(2)}) copy-start(bf16[32,96,256]{2,1,0:T(8,128)(2,1)} %param.10) | copy-start | bytes 4718596
  54.4 38.1 %copy-start.1 = (bf16[256,256]{1,0:T(8,128)(2,1)S(1)}, bf16[256,256]{1,0:T(8,128)(2,1)}, u32[]{:S(2)}) copy-start(bf16[256,256]{1,0:T(8,128)(2,1)} %param.8) | copy-start | bytes 393220
  54.4 3.6 %collective-permute-start = (f32[256,256]{0,1:T(8,128)S(1)}, f32[256,256]{0,1:T(8,128)S(1)}, u32[]{:S(2)}, u32[]{:S(2)}) collective-permute-start(f32[256,256]{0,1:T(8,128)S(1)} %convolution_bitcast_fusion.1), channel_id=1, source_target_pairs={{0,32},{32,0},{64,96},{96,64},{128,160},{160,128},{192,224},{224,1... | collective-permute-start | bytes 786440 | tf_op jit(solution)/shard_map/ppermute | solution.py:28
  58.0 10.2 %collective-permute-start.1 = (f32[256,256]{0,1:T(8,128)S(1)}, f32[256,256]{0,1:T(8,128)S(1)}, u32[]{:S(2)}, u32[]{:S(2)}) collective-permute-start(f32[256,256]{0,1:T(8,128)S(1)} %add.19), channel_id=1, source_target_pairs={{0,64},{32,96},{64,0},{96,32},{128,192},{160,224},{192,128},{224,1... | collective-permute-start | bytes 786440 | tf_op jit(solution)/shard_map/ppermute | solution.py:28
  68.3 15.9 %collective-permute-start.2 = (f32[256,256]{0,1:T(8,128)S(1)}, f32[256,256]{0,1:T(8,128)S(1)}, u32[]{:S(2)}, u32[]{:S(2)}) collective-permute-start(f32[256,256]{0,1:T(8,128)S(1)} %add.20), channel_id=1, source_target_pairs={{0,128},{32,160},{64,192},{96,224},{128,0},{160,32},{192,64},{224,... | collective-permute-start | bytes 786440 | tf_op jit(solution)/shard_map/ppermute | solution.py:28
  84.3 20.4 %collective-permute-start.3 = (f32[256,256]{0,1:T(8,128)S(1)}, f32[256,256]{0,1:T(8,128)S(1)}, u32[]{:S(2)}, u32[]{:S(2)}) collective-permute-start(f32[256,256]{0,1:T(8,128)S(1)} %add.21), channel_id=1, source_target_pairs={{0,256},{32,288},{64,320},{96,352},{128,384},{160,416},{192,448},{... | collective-permute-start | bytes 786440 | tf_op jit(solution)/shard_map/ppermute | solution.py:28
  106.4 44.4 %all-to-all-start.1 = ((bf16[32,96,256]{2,1,0:T(8,128)(2,1)}), bf16[32,96,256]{2,1,0:T(8,128)(2,1)S(1)}, u32[]{:S(2)}, u32[]{:S(2)}) async-start(bf16[32,96,256]{2,1,0:T(8,128)(2,1)} %fusion), calls=%async_computation.1 | async-start | bytes 3145728 | tf_op jit(solution)/shard_map/all_to_all | solution.py:36
  150.9 1.4 copy-start.2
